TPU v7x, 256 devices: a whole 4x4x8 slice. The times are simulated.
256 devices in a mesh: replica: 8 (over z), fsdp: 32 (over x, y, core).
Axes of the slice: x: 4, y: 4, z: 8, core: 2. Of those that a mesh axis runs over, the one named last changes fastest.
Arguments:
- grad_parts: bfloat16 [8, 256, 512, 512], P('replica', None, 'fsdp'), may hold values from -6 to 6
- moment: float32 [256, 512, 512], P(('replica', 'fsdp')), may hold values from -4 to 4
- second_moment: float32 [256, 512, 512], P(('replica', 'fsdp')), may hold values from 0.25 to 4
- left_factor: float32 [256, 512, 512], P(('replica', 'fsdp'))
- right_factor: float32 [256, 512, 512], P(('replica', 'fsdp'))
- left_basis: float32 [256, 512, 512], P(('replica', 'fsdp'))
- right_basis: float32 [256, 512, 512], P(('replica', 'fsdp'))
- block_order: int32 [256], replicated, may hold values from 0 to 255, as said below
- refresh_ids: int32 [25], replicated, may hold values from 0 to 249, as said below
Outputs:
- step_dir: bfloat16 [256, 512, 512], P('replica', 'fsdp')
- left_new: float32 [256, 512, 512], P(('replica', 'fsdp'))
- right_new: float32 [256, 512, 512], P(('replica', 'fsdp'))
Inputs may be any that keep to these rules, and one draw needn't show every extreme that they name: Slot s holds block block_order[s]; it is a permutation of the 256 blocks in which block_order[s] // 32 == s // 32. refresh_ids[j] lies in [10 j, 10 j + 9]; the ids are distinct and rising; the first is 0 and the last is 249.
All inputs are finite; a program needn't handle non-finite values.
Results may differ from a plain program's by a relative error of at most 0.011.
Values may be sent and summed in bfloat16 or wider, within the bound.
A program may use at most 128 MiB of HBM per device.

v0:
```python
import jax
import jax.numpy as jnp
from jax import lax
from jax.sharding import PartitionSpec as P

highest = lax.Precision.HIGHEST


def orthonormal(product):
    gram = jnp.dot(product.T, product, precision=highest)
    lower = jnp.linalg.cholesky(gram)
    return jax.scipy.linalg.solve_triangular(lower, product.T, lower=True).T


def refresh_bases(factor, basis, refresh_flags):

    def single(items):
        factor_one, basis_one, flag_one = items
        return lax.cond(
            flag_one,
            lambda: orthonormal(jnp.dot(factor_one, basis_one, precision=highest)),
            lambda: basis_one,
        )

    return lax.map(single, (factor, basis, refresh_flags))


def soap_update(gradient, moment, second_moment, left_q, right_q):
    moment_next = 0.9 * moment + 0.1 * gradient
    rot_grad = jnp.einsum(
        "kil,klm->kim",
        jnp.einsum("kji,kjl->kil", left_q, gradient, precision=highest),
        right_q,
        precision=highest,
    )
    rot_moment = jnp.einsum(
        "kil,klm->kim",
        jnp.einsum("kji,kjl->kil", left_q, moment_next, precision=highest),
        right_q,
        precision=highest,
    )
    second_next = 0.95 * second_moment + 0.05 * rot_grad * rot_grad
    scaled = rot_moment / (jnp.sqrt(second_next) + 1e-08)
    back = jnp.einsum("kil,klm->kim", left_q, scaled, precision=highest)
    return jnp.einsum("kim,knm->kin", back, right_q, precision=highest)


def on_device(
    grad_parts,
    moment,
    second_moment,
    left_factor,
    right_factor,
    left_basis,
    right_basis,
    block_order,
    refresh_ids,
):
    replicas = lax.axis_size("replica")
    replica_at = lax.axis_index("replica")
    owner_at = lax.axis_index("fsdp")
    total_blocks = grad_parts.shape[1]
    group_size = total_blocks // replicas
    per_owner = moment.shape[0]
    block_width = moment.shape[2]
    group_start = replica_at * group_size
    local_order = lax.dynamic_slice_in_dim(block_order, group_start, group_size) - group_start
    arranged = jnp.take(grad_parts, block_order, axis=1)
    partials = lax.all_to_all(
        lax.all_to_all(arranged, "replica", split_axis=1, concat_axis=0, tiled=True),
        "fsdp",
        split_axis=1,
        concat_axis=2,
        tiled=True,
    )
    gradient = jnp.sum(partials, axis=0, dtype=jnp.float32)
    slot_blocks = lax.dynamic_slice_in_dim(
        block_order, group_start + owner_at * per_owner, per_owner
    )
    own_flags = jnp.any(slot_blocks[:, None] == refresh_ids[None, :], axis=1)
    left_new = (
        0.95 * left_factor
        + 0.05 * jnp.einsum("kij,klj->kil", gradient, gradient, precision=highest) / block_width
    )
    right_new = (
        0.95 * right_factor
        + 0.05 * jnp.einsum("kji,kjl->kil", gradient, gradient, precision=highest) / block_width
    )
    left_next = refresh_bases(left_new, left_basis, own_flags)
    right_next = refresh_bases(right_new, right_basis, own_flags)
    update = soap_update(gradient, moment, second_moment, left_next, right_next).astype(
        jnp.bfloat16
    )
    returned = lax.all_to_all(update, "fsdp", split_axis=1, concat_axis=0, tiled=True)
    positions = (
        jnp.zeros((group_size,), jnp.int32)
        .at[local_order]
        .set(jnp.arange(group_size, dtype=jnp.int32))
    )
    return (jnp.take(returned, positions, axis=0), left_new, right_new)


def solution(mesh):
    placed = (
        P("replica", None, "fsdp", None),
        P(("replica", "fsdp"), None, None),
        P(("replica", "fsdp"), None, None),
        P(("replica", "fsdp"), None, None),
        P(("replica", "fsdp"), None, None),
        P(("replica", "fsdp"), None, None),
        P(("replica", "fsdp"), None, None),
        P(),
        P(),
    )
    return jax.shard_map(
        on_device,
        mesh=mesh,
        in_specs=placed,
        out_specs=(
            P("replica", "fsdp", None),
            P(("replica", "fsdp"), None, None),
            P(("replica", "fsdp"), None, None),
        ),
        check_vma=False,
    )
```

profile of v0, /device:TPU:1, one launch (start us, length us, event | category | flops | bytes accessed | tf_op | source)
XLA Modules:
  0.0 551.2 jit_solution(4676608241020184034)
XLA Ops:
  2.0 4.9 gather_fusion
  6.9 2.7 bitcast_select_fusion
  9.7 103.5 %all_to_all.33 = bf16[1,256,16,512]{3,2,0,1:T(8,128)(2,1)S(1)} all-to-all(bf16[1,256,16,512]{3,2,0,1:T(8,128)(2,1)S(1)} %bitcast_select_fusion), channel_id=1, replica_groups=mesh['replica'=8,'fsdp'=32] {'replica'}, dimensions={1} | all-to-all | bytes 8388608 | tf_op jit(solution)/shard_map/all_to_all | solution.py:70
  113.1 2.4 copy.43
  115.5 9.7 %all-to-all-start.1 = ((bf16[8,32,16,512]{3,2,0,1:T(8,128)(2,1)}), bf16[8,32,16,512]{3,2,0,1:T(8,128)(2,1)}, u32[]{:S(2)}, u32[]{:S(2)}) async-start(bf16[8,32,16,512]{3,2,0,1:T(8,128)(2,1)} %copy.43), calls=%async_computation.1 | async-start | bytes 8388608 | tf_op jit(solution)/shard_map/all_to_all | solution.py:69
  125.9 1.3 compare_reduce_fusion.8
  128.6 48.9 %all-to-all-done.1 = bf16[8,32,16,512]{3,2,0,1:T(8,128)(2,1)} async-done(((bf16[8,32,16,512]{3,2,0,1:T(8,128)(2,1)}), bf16[8,32,16,512]{3,2,0,1:T(8,128)(2,1)}, u32[]{:S(2)}, u32[]{:S(2)}) %all-to-all-start.1) | async-done | bytes 4194336 | tf_op jit(solution)/shard_map/all_to_all | solution.py:69
  177.5 3.2 convert_reduce_fusion
  180.7 1.2 broadcast_multiply_fusion
  181.9 2.9 fusion.68
  184.8 2.9 fusion.67
  187.6 4.0 conditional.2
  191.7 2.8 fusion.93
  194.5 1.8 bitcast_add_fusion.2
  196.3 2.9 fusion.78
  199.2 10.6 %conditional.3 = (f32[512,512]{0,1:T(8,128)S(1)}) conditional(s32[]{:T(128)} %convert_element_type.19, (f32[512,512]{1,0:T(8,128)S(1)}) %tuple.90, (f32[1,512,512]{2,1,0:T(8,128)}, f32[512,512]{1,0:T(8,128)S(1)}) %tuple.91), branch_computations={%region_13.16_spmd, %region_14.17_spmd} | conditional | flops 4633986048 | bytes 29889808 | solution.py:19
  209.8 3.2 fusion.94
  213.0 3.1 convolution_bitcast_fusion
  216.1 2.3 fusion.76
  218.4 1.9 fusion.69
  221.6 3.8 reduce.22
  225.4 1.2 reshape.198
  226.6 310.7 %all-to-all-start.2 = ((bf16[32,2,4096]{2,1,0:T(2,128)(2,1)}), bf16[32,2,4096]{2,1,0:T(2,128)(2,1)S(1)}, u32[]{:S(2)}, u32[]{:S(2)}) async-start(bf16[32,2,4096]{2,1,0:T(2,128)(2,1)} %reshape.198), calls=%async_computation.2 | async-start | bytes 1048576 | tf_op jit(solution)/shard_map/all_to_all | solution.py:94
  537.3 11.6 %all-to-all-done.2 = bf16[32,2,4096]{2,1,0:T(2,128)(2,1)S(1)} async-done(((bf16[32,2,4096]{2,1,0:T(2,128)(2,1)}), bf16[32,2,4096]{2,1,0:T(2,128)(2,1)S(1)}, u32[]{:S(2)}, u32[]{:S(2)}) %all-to-all-start.2) | async-done | bytes 524320 | tf_op jit(solution)/shard_map/all_to_all | solution.py:94
  (32 shorter events, 6.9 us)
Async XLA Ops:
  115.5 9.8 %copy-start.5 = (s32[256]{0:T(256)S(1)}, s32[256]{0:T(256)}, u32[]{:S(2)}) copy-start(s32[256]{0:T(256)} %param.23) | copy-start | bytes 3076
  115.5 10.4 %copy-start.8 = (s32[25]{0:T(128)S(1)}, s32[25]{0:T(128)}, u32[]{:S(2)}) copy-start(s32[25]{0:T(128)} %param.24) | copy-start | bytes 304
  115.5 61.9 %all-to-all-start.1 = ((bf16[8,32,16,512]{3,2,0,1:T(8,128)(2,1)}), bf16[8,32,16,512]{3,2,0,1:T(8,128)(2,1)}, u32[]{:S(2)}, u32[]{:S(2)}) async-start(bf16[8,32,16,512]{3,2,0,1:T(8,128)(2,1)} %copy.43), calls=%async_computation.1 | async-start | bytes 8388608 | tf_op jit(solution)/shard_map/all_to_all | solution.py:69
  125.3 56.6 %copy-start.4 = (f32[1,512,512]{2,1,0:T(8,128)S(1)}, f32[1,512,512]{2,1,0:T(8,128)}, u32[]{:S(2)}) copy-start(f32[1,512,512]{2,1,0:T(8,128)} %param.19) | copy-start | bytes 3145732
  180.7 4.1 copy-start.6
  184.8 2.9 copy-start
  191.7 4.6 copy-start.1
  209.8 6.3 %copy-start.7 = (f32[1,512,512]{2,1,0:T(8,128)S(1)}, f32[1,512,512]{2,1,0:T(8,128)}, u32[]{:S(2)}) copy-start(f32[1,512,512]{2,1,0:T(8,128)} %param.18) | copy-start | bytes 3145732
  226.6 322.3 %all-to-all-start.2 = ((bf16[32,2,4096]{2,1,0:T(2,128)(2,1)}), bf16[32,2,4096]{2,1,0:T(2,128)(2,1)S(1)}, u32[]{:S(2)}, u32[]{:S(2)}) async-start(bf16[32,2,4096]{2,1,0:T(2,128)(2,1)} %reshape.198), calls=%async_computation.2 | async-start | bytes 1048576 | tf_op jit(solution)/shard_map/all_to_all | solution.py:94
where the time goes:
time: 559 us; the launch traced here: 551 us
  starting transfers between devices  320 us (57%)
  blocking collectives  103 us (18%)
  waiting for transfers between devices  60.5 us (11%)
  matrix products  21.9 us (4%)
  other arithmetic  16.3 us (3%)
  loops' own time  14 us (3%)
  local copies, waits for them, and re-layouts  13.1 us (2%)
    all_to_all x1, starting transfers between devices, on_device(): lax.all_to_all(update, 'fsdp', split_axis=1, concat_axis=0, tiled=True)  311 us
    all_to_all x1, blocking collectives, on_device(): lax.all_to_all(arranged, 'replica', split_axis=1, concat_axis=0, tiled=True)  103 us
    all_to_all x1, waiting for transfers between devices, on_device(): lax.all_to_all(lax.all_to_all(arranged, 'replica', split_axis=1, concat_a...  48.9 us
    another operation x2, loops' own time, single(): lax.cond(flag_one, lambda: orthonormal(jnp.dot(factor_one, basis_one, pre...  14 us
    all_to_all x1, waiting for transfers between devices, on_device(): lax.all_to_all(update, 'fsdp', split_axis=1, concat_axis=0, tiled=True)  11.6 us
  transfers between devices with their start and end apart: 2, of which 2 were waited for; matrix products, arithmetic and copies ran while one was open for 0% of the time, Pallas kernels for 0%

commit v1 on v0

v1 whole, which is shorter than its diff:
```python
import functools

import jax
import jax.numpy as jnp
from jax import lax
from jax.experimental import pallas as pl
from jax.experimental.pallas import tpu as pltpu
from jax.sharding import PartitionSpec as P

MESH = pl.DeviceIdType.MESH
f32 = jnp.float32
bf16 = jnp.bfloat16

PIECES = 4
DOWN, UP = 0, 1
LONG, SHORT = 0, 1
HOPS = (4, 3)


def greet(partners):
    barrier = pltpu.get_barrier_semaphore()
    for partner in partners:
        pl.semaphore_signal(barrier, inc=1, device_id=partner, device_id_type=MESH)


def gather_kernel(nz, nf, order_ref, parts_ref, grad_ref, own, first, arms, out, load_sem,
                  arm_send, arm_recv, out_send, out_recv):
    z = lax.axis_index("replica")
    f = lax.axis_index("fsdp")
    group = own.shape[0] // nz
    half = group // 2
    per = half // PIECES
    rows = own.shape[1]

    loads = [
        pltpu.make_async_copy(
            parts_ref.at[0, pl.ds(g * group, group)], own.at[pl.ds(g * group, group)], load_sem.at[g]
        )
        for g in range(nz)
    ]
    for load in loads:
        load.start()

    barrier = pltpu.get_barrier_semaphore()
    for step in (1, nz - 1):
        pl.semaphore_signal(
            barrier, inc=1, device_id=(lax.rem(z + step, nz), f), device_id_type=MESH
        )

    def hello(i, c):
        pl.semaphore_signal(
            barrier, inc=1, device_id=(z, lax.rem(f + i, nf)), device_id_type=MESH
        )
        return c

    lax.fori_loop(1, nf, hello, 0)
    for load in loads:
        load.wait()
    pl.semaphore_wait(barrier, nf + 1)

    def mine(dest, i):
        slot = lax.rem(f + i, nf)
        return own[order_ref[dest * group + slot]]

    def half_of(way, arm):
        return way ^ arm

    def copy(way, arm, hop, p):
        src = first.at[way, arm] if hop == 0 else arms.at[way, arm, hop - 1]
        step = nz - 1 if way == DOWN else 1
        piece = pl.ds(p * per, per)
        return pltpu.make_async_remote_copy(
            src_ref=src.at[piece],
            dst_ref=arms.at[way, arm, hop].at[piece],
            send_sem=arm_send.at[way, arm, hop, p],
            recv_sem=arm_recv.at[way, arm, hop, p],
            device_id=(lax.rem(z + step, nz), f),
            device_id_type=MESH,
        )

    def target(way, arm, hop):
        left = HOPS[arm] - hop
        return lax.rem(z + (nz - left if way == DOWN else left), nz)

    for hop in range(4):

        def piece_step(p, c):
            for arm in (LONG, SHORT):
                if hop >= HOPS[arm]:
                    continue
                for way in (DOWN, UP):
                    if hop > 0:
                        copy(way, arm, hop - 1, p).wait_recv()
                    dest = target(way, arm, hop)
                    start = half_of(way, arm) * half

                    def slot_step(k, c):
                        i = p * per + k
                        value = mine(dest, start + i)
                        if hop == 0:
                            first[way, arm, i] = value
                        else:
                            total = arms[way, arm, hop - 1, i].astype(f32) + value.astype(f32)
                            arms[way, arm, hop - 1, i] = total.astype(bf16)
                        return c

                    lax.fori_loop(0, per, slot_step, 0)
                    copy(way, arm, hop, p).start()
            return c

        lax.fori_loop(0, PIECES, piece_step, 0)

    def send_out(i):
        peer = lax.rem(f + i, nf)
        return pltpu.make_async_remote_copy(
            src_ref=out.at[i],
            dst_ref=grad_ref.at[pl.ds(pl.multiple_of(f * rows, rows), rows)],
            send_sem=out_send.at[i],
            recv_sem=out_recv.at[i],
            device_id=(z, peer),
            device_id_type=MESH,
        )

    def finish(p, c):
        for part in range(2):
            long_way = DOWN if part == 0 else UP
            short_way = UP if part == 0 else DOWN
            copy(long_way, LONG, 3, p).wait_recv()
            copy(short_way, SHORT, 2, p).wait_recv()

            def slot_step(k, c):
                i = p * per + k
                total = (
                    arms[long_way, LONG, 3, i].astype(f32)
                    + arms[short_way, SHORT, 2, i].astype(f32)
                    + mine(z, part * half + i).astype(f32)
                ).astype(bf16)
                j = part * half + i
                out[j] = total

                @pl.when(j == 0)
                def _():
                    grad_ref[pl.ds(pl.multiple_of(f * rows, rows), rows)] = total

                @pl.when(j > 0)
                def _():
                    send_out(j).start()

                return c

            lax.fori_loop(0, per, slot_step, 0)
        return c

    lax.fori_loop(0, PIECES, finish, 0)

    def drain(i, c):
        send_out(i).wait_send()
        send_out(i).wait_recv()
        return c

    lax.fori_loop(1, nf, drain, 0)

    for hop in range(4):
        for arm in (LONG, SHORT):
            if hop < HOPS[arm]:
                for way in (DOWN, UP):

                    def sent(p, c):
                        copy(way, arm, hop, p).wait_send()
                        return c

                    lax.fori_loop(0, PIECES, sent, 0)


def gather(nz, nf, order, parts):
    _, blocks, rows, width = parts.shape
    half = blocks // nz // 2
    return pl.pallas_call(
        functools.partial(gather_kernel, nz, nf),
        out_shape=jax.ShapeDtypeStruct((nf * rows, width), bf16),
        in_specs=[
            pl.BlockSpec(memory_space=pltpu.SMEM),
            pl.BlockSpec(memory_space=pl.ANY),
        ],
        out_specs=pl.BlockSpec(memory_space=pltpu.VMEM),
        scratch_shapes=[
            pltpu.VMEM((blocks, rows, width), bf16),
            pltpu.VMEM((2, 2, half, rows, width), bf16),
            pltpu.VMEM((2, 2, 4, half, rows, width), bf16),
            pltpu.VMEM((2 * half, rows, width), bf16),
            pltpu.SemaphoreType.DMA((nz,)),
            pltpu.SemaphoreType.DMA((2, 2, 4, PIECES)),
            pltpu.SemaphoreType.DMA((2, 2, 4, PIECES)),
            pltpu.SemaphoreType.DMA((nf,)),
            pltpu.SemaphoreType.DMA((nf,)),
        ],
        compiler_params=pltpu.CompilerParams(
            collective_id=0, has_side_effects=True, vmem_limit_bytes=40 * 2**20
        ),
        name="gather_grad",
    )(order, parts)


NB = 64


def split(x):
    high = x.astype(bf16)
    return high, (x - high.astype(f32)).astype(bf16)


def dg(a, b, ca, cb):
    return lax.dot_general(a, b, (((ca,), (cb,)), ((), ())), preferred_element_type=f32)


def dot3(a, b, ca=1, cb=0):
    return dg(a[0], b[0], ca, cb) + (dg(a[0], b[1], ca, cb) + dg(a[1], b[0], ca, cb))


def lanes(x, at):
    return [
        jnp.take_along_axis(x, jnp.full(x.shape, at + j, jnp.int32), axis=1) for j in range(8)
    ]


def spread(x, j):
    return jnp.broadcast_to(x[j : j + 1, :], x.shape)


def pivot_rows(e_ref, m, at):
    sub = lax.broadcasted_iota(jnp.int32, (8, 128), 0)
    piv = e_ref[m, at : at + 8, :]
    b = lanes(piv, at)
    diag = None
    inverse, above, pivots = [], [], []
    for j in range(8):
        d = spread(b[j], j)
        diag = d if diag is None else jnp.where(sub == j, d, diag)
        r = 1.0 / d
        inverse.append(r)
        factor = jnp.where(sub > j, b[j] * r, 0.0)
        row = {}
        for t in range(j + 1, 8):
            row[t] = spread(b[t], j)
            b[t] = b[t] - factor * row[t]
        above.append(row)
        pivots.append(spread(piv, j))
        piv = piv - factor * pivots[j]
    return inverse, above, pivots, piv * lax.rsqrt(diag)


def chol_inverse(e_ref):
    for at in range(0, NB, 8):
        found = [pivot_rows(e_ref, m, at) for m in range(2)]
        for m in range(2):
            inverse, above, pivots, piv = found[m]
            for i in range(at + 8, NB, 8):
                x = e_ref[m, i : i + 8, :]
                b = lanes(x, at)
                for j in range(8):
                    factor = b[j] * inverse[j]
                    for t in range(j + 1, 8):
                        b[t] = b[t] - factor * above[j][t]
                    x = x - factor * pivots[j]
                e_ref[m, i : i + 8, :] = x
            e_ref[m, at : at + 8, :] = piv


def orthonormal(a_ref, t_ref, e_ref):
    size = a_ref.shape[1]
    eye = (
        lax.broadcasted_iota(jnp.int32, (NB, NB), 0) == lax.broadcasted_iota(jnp.int32, (NB, NB), 1)
    ).astype(f32)
    for o in range(0, size, NB):
        n = o + NB
        for m in range(2):
            e_ref[m, :, :NB] = a_ref[m, o:n, o:n]
            e_ref[m, :, NB:] = eye
        chol_inverse(e_ref)
        for m in range(2):
            w = split(e_ref[m, :, NB:])
            t = dot3(w, split(t_ref[m, o:n, :]))
            t_ref[m, o:n, :] = t
            if n < size:
                u = split(dot3(w, split(a_ref[m, o:n, n:])))
                a_ref[m, n:, n:] = a_ref[m, n:, n:] - dot3(u, u, 0, 0)
                t_ref[m, n:, :] = t_ref[m, n:, :] - dot3(u, split(t), 0, 0)


def step_kernel(order_ref, ids_ref, grad_ref, mom_hbm, sec_hbm, lf_hbm, rf_hbm, lb_hbm, rb_hbm,
                update_ref, ln_hbm, rn_hbm, mom, sec, fac, bas, new, a_ref, t_ref, e_ref,
                in_sem, out_sem):
    nf = 32
    slot = lax.axis_index("replica") * nf + lax.axis_index("fsdp")
    width = grad_ref.shape[1]
    loads = [
        pltpu.make_async_copy(src.at[0], dst, in_sem.at[n])
        for n, (src, dst) in enumerate(
            (
                (lf_hbm, fac.at[0]),
                (rf_hbm, fac.at[1]),
                (lb_hbm, bas.at[0]),
                (rb_hbm, bas.at[1]),
                (mom_hbm, mom),
                (sec_hbm, sec),
            )
        )
    ]
    for load in loads:
        load.start()
    block = order_ref[slot]
    flag = lax.fori_loop(
        0, ids_ref.shape[0], lambda i, c: c | (ids_ref[i] == block).astype(jnp.int32), jnp.int32(0)
    )
    grad = grad_ref[...]
    stores = []
    for m, hbm in enumerate((ln_hbm, rn_hbm)):
        loads[m].wait()
        new[m] = 0.95 * fac[m] + (0.05 / width) * dg(grad, grad, 1 - m, 1 - m)
        stores.append(pltpu.make_async_copy(new.at[m], hbm.at[0], out_sem.at[m]))
        stores[m].start()
    loads[2].wait()
    loads[3].wait()

    @pl.when(flag == 1)
    def _():
        for m in range(2):
            t = dot3(split(bas[m]), split(new[m]), 0, 1)
            t_ref[m] = t
            s = split(t)
            a_ref[m] = dot3(s, s, 1, 1)
        orthonormal(a_ref, t_ref, e_ref)
        for m in range(2):
            bas[m] = t_ref[m].T

    loads[4].wait()
    loads[5].wait()
    lq = split(bas[0])
    rq = split(bas[1])
    moment = split(0.9 * mom[...] + 0.1 * grad.astype(f32))
    half_grad = split(dg(lq[0], grad, 0, 0) + dg(lq[1], grad, 0, 0))
    half_mom = split(dot3(lq, moment, 0, 0))
    rot_grad = dot3(half_grad, rq)
    rot_mom = dot3(half_mom, rq)
    second = 0.95 * sec[...] + 0.05 * rot_grad * rot_grad
    scaled = split(rot_mom / (jnp.sqrt(second) + 1e-08))
    back = split(dot3(lq, scaled))
    update_ref[...] = dot3(back, rq, 1, 1).astype(bf16)
    for store in stores:
        store.wait()


def step(order, ids, grad, moment, second, lf, rf, lb, rb):
    width = grad.shape[1]
    square = pltpu.VMEM((width, width), f32)
    pair = pltpu.VMEM((2, width, width), f32)
    smem = pl.BlockSpec(memory_space=pltpu.SMEM)
    vmem = pl.BlockSpec(memory_space=pltpu.VMEM)
    hbm = pl.BlockSpec(memory_space=pl.ANY)
    whole = jax.ShapeDtypeStruct((1, width, width), f32)
    return pl.pallas_call(
        step_kernel,
        out_shape=(jax.ShapeDtypeStruct((width, width), bf16), whole, whole),
        in_specs=[smem, smem, vmem] + [hbm] * 6,
        out_specs=(vmem, hbm, hbm),
        scratch_shapes=[
            square,
            square,
            pair,
            pair,
            pair,
            pair,
            pair,
            pltpu.VMEM((2, NB, 2 * NB), f32),
            pltpu.SemaphoreType.DMA((6,)),
            pltpu.SemaphoreType.DMA((2,)),
        ],
        compiler_params=pltpu.CompilerParams(vmem_limit_bytes=50 * 2**20),
        name="block_step",
    )(order, ids, grad, moment, second, lf, rf, lb, rb)


def scatter_kernel(nf, where_ref, update_ref, out_ref, held, send_sem, recv_sem):
    z = lax.axis_index("replica")
    f = lax.axis_index("fsdp")
    rows = out_ref.shape[1]
    barrier = pltpu.get_barrier_semaphore()

    def hello(i, c):
        pl.semaphore_signal(
            barrier, inc=1, device_id=(z, lax.rem(f + i, nf)), device_id_type=MESH
        )
        return c

    lax.fori_loop(1, nf, hello, 0)
    pl.semaphore_wait(barrier, nf - 1)

    def copy(i):
        peer = lax.rem(f + i, nf)
        return pltpu.make_async_remote_copy(
            src_ref=update_ref.at[pl.ds(pl.multiple_of(peer * rows, rows), rows)],
            dst_ref=held.at[f],
            send_sem=send_sem.at[i],
            recv_sem=recv_sem.at[i],
            device_id=(z, peer),
            device_id_type=MESH,
        )

    def begin(i, c):
        copy(i).start()
        return c

    def drain(i, c):
        copy(i).wait()
        return c

    def place(i, c):
        out_ref[i] = held[where_ref[i]]
        return c

    lax.fori_loop(1, nf, begin, 0)
    held[f] = update_ref[pl.ds(pl.multiple_of(f * rows, rows), rows)]
    lax.fori_loop(1, nf, drain, 0)
    lax.fori_loop(0, nf, place, 0)


def scatter(nf, where, update):
    width = update.shape[1]
    rows = update.shape[0] // nf
    return pl.pallas_call(
        functools.partial(scatter_kernel, nf),
        out_shape=jax.ShapeDtypeStruct((nf, rows, width), bf16),
        in_specs=[
            pl.BlockSpec(memory_space=pltpu.SMEM),
            pl.BlockSpec(memory_space=pltpu.VMEM),
        ],
        out_specs=pl.BlockSpec(memory_space=pltpu.VMEM),
        scratch_shapes=[
            pltpu.VMEM((nf, rows, width), bf16),
            pltpu.SemaphoreType.DMA((nf,)),
            pltpu.SemaphoreType.DMA((nf,)),
        ],
        compiler_params=pltpu.CompilerParams(collective_id=1, has_side_effects=True),
        name="scatter_update",
    )(where, update)


def solution(mesh):
    nz, nf = mesh.shape["replica"], mesh.shape["fsdp"]

    def on_device(parts, moment, second, lf, rf, lb, rb, order, ids):
        group = parts.shape[1] // nz
        start = lax.axis_index("replica") * group
        local = lax.dynamic_slice_in_dim(order, start, group) - start
        blocks = jnp.arange(group, dtype=jnp.int32)
        where = jnp.sum(jnp.where(local[None, :] == blocks[:, None], blocks[None, :], 0), axis=1)
        grad = gather(nz, nf, order, parts)
        update, left_new, right_new = step(order, ids, grad, moment, second, lf, rf, lb, rb)
        return scatter(nf, where, update), left_new, right_new

    placed = (P("replica", None, "fsdp", None),) + (P(("replica", "fsdp"), None, None),) * 6 + (P(), P())
    return jax.shard_map(
        on_device,
        mesh=mesh,
        in_specs=placed,
        out_specs=(
            P("replica", "fsdp", None),
            P(("replica", "fsdp"), None, None),
            P(("replica", "fsdp"), None, None),
        ),
        check_vma=False,
    )
```

time: 559 us -> 116 us (0.21); the launches traced: 551 us -> 116 us
  starting transfers between devices: 320 us -> 0 us
  Pallas kernels: 0 us -> 108 us
  blocking collectives: 103 us -> 0 us
  waiting for transfers between devices: 60.5 us -> 0 us
  matrix products: 21.9 us -> 0 us
  other arithmetic: 16.3 us -> 1.5 us
  loops' own time: 14 us -> 0 us
  local copies, waits for them, and re-layouts: 13.1 us -> 5.54 us
    all_to_all x2 -> x0, starting transfers between devices: 320 us -> none  [the longest x1 311 us: on_device(): lax.all_to_all(update, 'fsdp', split_axis=1, concat_axis=0, tiled=True)]
    pallas_call x0 -> x3, Pallas kernels: none -> 108 us  [the longest x1 60.2 us: gather(): pl.pallas_call(functools.partial(gather_kernel, nz, nf), out_shape=jax.Sh...]
    all_to_all x1 -> x0, blocking collectives: 103 us -> none  [on_device(): lax.all_to_all(arranged, 'replica', split_axis=1, concat_axis=0, tiled=True)]
    all_to_all x2 -> x0, waiting for transfers between devices: 60.5 us -> none  [the longest x1 48.9 us: on_device(): lax.all_to_all(lax.all_to_all(arranged, 'replica', split_axis=1, concat_a...]
    dot_general x8 -> x0, matrix products: 21.9 us -> none  [the longest x1 3.17 us: soap_update(): jnp.einsum('kil,klm->kim', jnp.einsum('kji,kjl->kil', left_q, gradient, p...]
    another operation x2 -> x0, loops' own time: 14 us -> none  [single(): lax.cond(flag_one, lambda: orthonormal(jnp.dot(factor_one, basis_one, pre...]
  transfers between devices with their start and end apart: 2 -> 0, of which waited for: 2 -> 0; matrix products, arithmetic and copies ran while one was open for 0% -> 0% of each run, Pallas kernels for 0% -> 0%
where the time goes in v1:
time: 116 us
  Pallas kernels  108 us (93%)
  local copies, waits for them, and re-layouts  5.54 us (5%)
  other arithmetic  1.5 us (1%)
    pallas_call x1, Pallas kernels, gather(): pl.pallas_call(functools.partial(gather_kernel, nz, nf), out_shape=jax.Sh...  60.2 us
    pallas_call x1, Pallas kernels, scatter(): pl.pallas_call(functools.partial(scatter_kernel, nf), out_shape=jax.Shape...  40.2 us
    pallas_call x1, Pallas kernels, step(): pl.pallas_call(step_kernel, out_shape=(jax.ShapeDtypeStruct((width, width...  8.03 us
    unnamed x15, local copies, waits for them, and re-layouts  5.54 us

profile of v1, /device:TPU:1, one launch (start us, length us, event | category | flops | bytes accessed | tf_op | source)
XLA Modules:
  0.0 116.2 jit_solution(1527498077874905555)
XLA Ops:
  0.6 0.0 copy-start.5
  0.6 0.0 copy-start.6
  0.7 0.8 dynamic-slice_subtract_fusion
  1.5 0.7 select_reduce_fusion.where_ref
  2.2 0.0 copy-start
  2.2 2.2 %copy-done = bf16[1,256,16,512]{3,2,1,0:T(8,128)(2,1)S(1)} copy-done((bf16[1,256,16,512]{3,2,1,0:T(8,128)(2,1)S(1)}, bf16[1,256,16,512]{3,2,1,0:T(8,128)(2,1)}, u32[]{:S(2)}) %copy-start) | copy-done | bytes 4194328
  4.3 0.0 copy-start.4
  4.3 0.7 copy-done.4
  5.0 0.0 copy-start.1
  5.0 0.0 copy-start.2
  5.0 60.2 %gather_grad.1.grad_ref = bf16[512,512]{1,0:T(8,128)(2,1)S(1)} custom-call(s32[256]{0:T(256)S(1)} %copy-done.4, bf16[1,256,16,512]{3,2,1,0:T(8,128)(2,1)S(1)} %copy-done), custom_call_target="tpu_custom_call" | custom-call | tf_op jit(solution)/shard_map/gather_grad/pallas_call | solution.py:178
  65.2 0.0 copy-done.5
  65.2 0.0 copy-done.6
  65.2 0.0 copy-done.1
  65.2 0.0 copy-done.2
  65.2 8.0 %block_step.1 = (bf16[512,512]{1,0:T(8,128)(2,1)S(1)}, f32[1,512,512]{2,1,0:T(8,128)}, f32[1,512,512]{2,1,0:T(8,128)}) custom-call(s32[256]{0:T(256)S(1)} %copy-done.5, s32[25]{0:T(128)S(1)} %copy-done.6, bf16[512,512]{1,0:T(8,128)(2,1)S(1)} %gather_grad.1.grad_ref, f32[1,512,512]{2,1,0:T(8,128)S(1)} %copy-done.1, f32[1,512,512]{2,1,0:T(8,128)S(1)} %copy-done.2, ...), custom_call_target="tpu_custom_call" | custom-call | tf_op jit(solution)/shard_map/block_step/pallas_call | solution.py:361
  73.3 0.0 copy-start.3
  73.3 0.8 copy-done.3
  74.1 40.2 %scatter_update.1 = bf16[32,16,512]{2,1,0:T(8,128)(2,1)} custom-call(s32[32]{0:T(128)} %select_reduce_fusion.where_ref, bf16[512,512]{1,0:T(8,128)(2,1)} %copy-done.3), custom_call_target="tpu_custom_call" | custom-call | tf_op jit(solution)/shard_map/scatter_update/pallas_call | solution.py:430
  114.3 1.9 %copy.13 = bf16[32,16,512]{2,1,0:T(8,128)(2,1)} copy(bf16[32,16,512]{2,1,0:T(8,128)(2,1)} %scatter_update.1) | data formatting | bytes 1048576
Async XLA Ops:
  0.6 64.6 %copy-start.5 = (s32[256]{0:T(256)S(1)}, s32[256]{0:T(256)}, u32[]{:S(2)}) copy-start(s32[256]{0:T(256)} %order_ref.3) | copy-start | bytes 3076
  0.6 64.6 %copy-start.6 = (s32[25]{0:T(128)S(1)}, s32[25]{0:T(128)}, u32[]{:S(2)}) copy-start(s32[25]{0:T(128)} %ids_ref.1) | copy-start | bytes 304
  2.2 2.2 %copy-start = (bf16[1,256,16,512]{3,2,1,0:T(8,128)(2,1)S(1)}, bf16[1,256,16,512]{3,2,1,0:T(8,128)(2,1)}, u32[]{:S(2)}) copy-start(bf16[1,256,16,512]{3,2,1,0:T(8,128)(2,1)} %parts_ref.1) | copy-start | bytes 12582916
  4.3 0.7 copy-start.4
  5.0 60.2 %copy-start.1 = (f32[1,512,512]{2,1,0:T(8,128)S(1)}, f32[1,512,512]{2,1,0:T(8,128)}, u32[]{:S(2)}) copy-start(f32[1,512,512]{2,1,0:T(8,128)} %mom_hbm.1) | copy-start | bytes 3145732
  5.0 60.2 %copy-start.2 = (f32[1,512,512]{2,1,0:T(8,128)S(1)}, f32[1,512,512]{2,1,0:T(8,128)}, u32[]{:S(2)}) copy-start(f32[1,512,512]{2,1,0:T(8,128)} %sec_hbm.1) | copy-start | bytes 3145732
  73.3 0.8 copy-start.3

commit v2 on v0

v2 whole, which is shorter than its diff:
```python
import functools

import jax
import jax.numpy as jnp
from jax import lax
from jax.experimental import pallas as pl
from jax.experimental.pallas import tpu as pltpu
from jax.sharding import PartitionSpec as P

MESH = pl.DeviceIdType.MESH
f32 = jnp.float32
bf16 = jnp.bfloat16

DOWN, UP = 0, 1
LONG, SHORT = 0, 1
HOPS = (4, 3)
EARLY = 4
DECADE = 10
PER = 2
NB = 64


def split(x):
    high = x.astype(bf16)
    return high, (x - high.astype(f32)).astype(bf16)


def dg(a, b, ca=1, cb=0):
    return lax.dot_general(a, b, (((ca,), (cb,)), ((), ())), preferred_element_type=f32)


def dot3(a, b, ca=1, cb=0):
    return dg(a[0], b[0], ca, cb) + (dg(a[0], b[1], ca, cb) + dg(a[1], b[0], ca, cb))


def lanes(x, at):
    return [
        jnp.take_along_axis(x, jnp.full(x.shape, at + j, jnp.int32), axis=1) for j in range(8)
    ]


def spread(x, j):
    return jnp.broadcast_to(x[j : j + 1, :], x.shape)


def pivot_rows(e_ref, m, at):
    sub = lax.broadcasted_iota(jnp.int32, (8, 128), 0)
    piv = e_ref[m, at : at + 8, :]
    b = lanes(piv, at)
    diag = None
    inverse, above, pivots = [], [], []
    for j in range(8):
        d = spread(b[j], j)
        diag = d if diag is None else jnp.where(sub == j, d, diag)
        r = 1.0 / d
        inverse.append(r)
        factor = jnp.where(sub > j, b[j] * r, 0.0)
        row = {}
        for t in range(j + 1, 8):
            row[t] = spread(b[t], j)
            b[t] = b[t] - factor * row[t]
        above.append(row)
        pivots.append(spread(piv, j))
        piv = piv - factor * pivots[j]
    return inverse, above, pivots, piv * lax.rsqrt(diag)


def chol_inverse(e_ref):
    for at in range(0, NB, 8):
        found = [pivot_rows(e_ref, m, at) for m in range(2)]
        for m in range(2):
            inverse, above, pivots, piv = found[m]
            for i in range(at + 8, NB, 8):
                x = e_ref[m, i : i + 8, :]
                b = lanes(x, at)
                for j in range(8):
                    factor = b[j] * inverse[j]
                    for t in range(j + 1, 8):
                        b[t] = b[t] - factor * above[j][t]
                    x = x - factor * pivots[j]
                e_ref[m, i : i + 8, :] = x
            e_ref[m, at : at + 8, :] = piv


def orthonormal(a_ref, t_ref, e_ref, between):
    size = a_ref.shape[1]
    eye = (
        lax.broadcasted_iota(jnp.int32, (NB, NB), 0) == lax.broadcasted_iota(jnp.int32, (NB, NB), 1)
    ).astype(f32)
    for o in range(0, size, NB):
        n = o + NB
        for m in range(2):
            e_ref[m, :, :NB] = a_ref[m, o:n, o:n]
            e_ref[m, :, NB:] = eye
        chol_inverse(e_ref)
        between()
        for m in range(2):
            w = split(e_ref[m, :, NB:])
            t = dot3(w, split(t_ref[m, o:n, :]))
            t_ref[m, o:n, :] = t
            if n < size:
                u = split(dot3(w, split(a_ref[m, o:n, n:])))
                a_ref[m, n:, n:] = a_ref[m, n:, n:] - dot3(u, u, 0, 0)
                t_ref[m, n:, :] = t_ref[m, n:, :] - dot3(u, split(t), 0, 0)
        between()


def main_kernel(
    nz, nf, order_ref, ids_ref, parts_hbm, mom_hbm, sec_hbm, lf_hbm, rf_hbm, lb_hbm, rb_hbm,
    held, grad,
    own, first_a, arms_a, first_b, arms_b, acc, out_a, grad_a, out_b, update,
    fac, bas, new, a_ref, t_ref, mom, sec, rotated, lq, rq, e_ref, back_hi,
    load_sem, send_a, recv_a, send_b, recv_b, give_a, take_a, give_b, take_b, give_c, take_c,
):
    z = lax.axis_index("replica")
    f = lax.axis_index("fsdp")
    group = own.shape[0] // nz
    rows, width = own.shape[1:]
    nref = ids_ref.shape[0]

    loads = [
        pltpu.make_async_copy(
            parts_hbm.at[0, pl.ds(g * group, group)], own.at[pl.ds(g * group, group)], load_sem.at[g]
        )
        for g in range(nz)
    ]
    places = (
        (lf_hbm, fac.at[0]),
        (rf_hbm, fac.at[1]),
        (lb_hbm, bas.at[0]),
        (rb_hbm, bas.at[1]),
        (mom_hbm, mom),
        (sec_hbm, sec),
    )
    later = [
        pltpu.make_async_copy(src.at[0], dst, load_sem.at[nz + n])
        for n, (src, dst) in enumerate(places)
    ]
    for load in loads + later:
        load.start()

    barrier = pltpu.get_barrier_semaphore()
    for step in (1, nz - 1):
        pl.semaphore_signal(
            barrier, inc=1, device_id=(lax.rem(z + step, nz), f), device_id_type=MESH
        )

    def hello(i, c):
        pl.semaphore_signal(
            barrier, inc=1, device_id=(z, lax.rem(f + i, nf)), device_id_type=MESH
        )
        return c

    lax.fori_loop(1, nf, hello, 0)

    def early(g):
        start = (g * group) // DECADE
        found = []
        for c in range(EARLY):
            at = start + c
            block = jnp.where(at < nref, ids_ref[jnp.minimum(at, nref - 1)], nz * group)
            found.append(jnp.clip(block - g * group, 0, group - 1))
        return found

    def late(found, q):
        block = q
        for a in found:
            block = block + (block >= a).astype(jnp.int32)
        return block

    own_early = early(z)

    def position(block):
        block = jnp.clip(block, 0, group - 1)
        below = sum((a < block).astype(jnp.int32) for a in own_early)
        same = sum((a == block).astype(jnp.int32) for a in own_early)
        return jnp.where(same > 0, below, EARLY + block - below)

    for load in loads:
        load.wait()
    pl.semaphore_wait(barrier, nf + 1)

    def target(way, arm, hop):
        left = HOPS[arm] - hop
        return lax.rem(z + (nz - left if way == DOWN else left), nz)

    def ring_copy(stage, way, arm, hop, p):
        first, arms, send, recv = stage
        src = first.at[way, arm] if hop == 0 else arms.at[way, arm, hop - 1]
        step = nz - 1 if way == DOWN else 1
        piece = pl.ds(p * PER, PER)
        return pltpu.make_async_remote_copy(
            src_ref=src.at[piece],
            dst_ref=arms.at[way, arm, hop].at[piece],
            send_sem=send.at[way, arm, hop, p],
            recv_sem=recv.at[way, arm, hop, p],
            device_id=(lax.rem(z + step, nz), f),
            device_id_type=MESH,
        )

    def block_at(stage, dest, part, i):
        found = early(dest)
        if stage is ring_a:
            return dest * group + found[part * (EARLY // 2) + i]
        return dest * group + late(found, part * ((group - EARLY) // 2) + i)

    def ring_step(stage, hop, p):
        first, arms = stage[:2]
        for arm in (LONG, SHORT):
            if hop >= HOPS[arm]:
                continue
            for way in (DOWN, UP):
                if hop > 0:
                    ring_copy(stage, way, arm, hop - 1, p).wait_recv()
                dest = target(way, arm, hop)
                for k in range(PER):
                    i = p * PER + k
                    value = own[block_at(stage, dest, way ^ arm, i)]
                    if hop == 0:
                        first[way, arm, i] = value
                    else:
                        total = arms[way, arm, hop - 1, i].astype(f32) + value.astype(f32)
                        arms[way, arm, hop - 1, i] = total.astype(bf16)
                ring_copy(stage, way, arm, hop, p).start()

    def ring_end(stage, p):
        arms = stage[1]
        base = 0 if stage is ring_a else EARLY
        count = EARLY // 2 if stage is ring_a else (group - EARLY) // 2
        for part in range(2):
            long_way, short_way = (DOWN, UP) if part == 0 else (UP, DOWN)
            ring_copy(stage, long_way, LONG, 3, p).wait_recv()
            ring_copy(stage, short_way, SHORT, 2, p).wait_recv()
            for k in range(PER):
                i = p * PER + k
                total = (
                    arms[long_way, LONG, 3, i].astype(f32)
                    + arms[short_way, SHORT, 2, i].astype(f32)
                    + own[block_at(stage, z, part, i)].astype(f32)
                )
                acc[base + part * count + i] = total.astype(bf16)

    def ring_sent(stage, pieces):
        for hop in range(4):
            for arm in (LONG, SHORT):
                if hop < HOPS[arm]:
                    for way in (DOWN, UP):

                        def sent(p, c):
                            ring_copy(stage, way, arm, hop, p).wait_send()
                            return c

                        lax.fori_loop(0, pieces, sent, 0)

    ring_a = (first_a, arms_a, send_a, recv_a)
    ring_b = (first_b, arms_b, send_b, recv_b)
    pieces = (group - EARLY) // 2 // PER
    todo = [functools.partial(ring_step, ring_b, hop, p) for hop in range(4) for p in range(pieces)]
    todo += [functools.partial(ring_end, ring_b, p) for p in range(pieces)]
    todo.reverse()

    def pump(n=1):
        for _ in range(n):
            if todo:
                todo.pop()()

    mine = pl.ds(pl.multiple_of(f * rows, rows), rows)

    def give(out, into, send, recv, i):
        return pltpu.make_async_remote_copy(
            src_ref=out.at[i],
            dst_ref=into.at[mine],
            send_sem=send.at[i],
            recv_sem=recv.at[i],
            device_id=(z, lax.rem(f + i, nf)),
            device_id_type=MESH,
        )

    def to_owners(out, into, send, recv, limit):
        def one(i, c):
            slot = lax.rem(f + i, nf)
            at = jnp.minimum(position(order_ref[z * group + slot] - z * group), limit)
            out[i] = acc[at]
            give(out, into, send, recv, i).start()
            return c

        lax.fori_loop(1, nf, one, 0)
        at = jnp.minimum(position(order_ref[z * group + f] - z * group), limit)
        into[mine] = acc[at]

    def from_all(out, into, send, recv):
        def one(i, c):
            give(out, into, send, recv, i).wait_recv()
            return c

        lax.fori_loop(1, nf, one, 0)

    ring_step(ring_a, 0, 0)
    pump(2)
    ring_step(ring_a, 1, 0)
    pump(1)
    ring_step(ring_a, 2, 0)
    pump(2)
    ring_step(ring_a, 3, 0)
    pump(2)
    ring_end(ring_a, 0)
    to_owners(out_a, grad_a, give_a, take_a, EARLY - 1)
    pump(4)
    for load in later:
        load.wait()
    from_all(out_a, grad_a, give_a, take_a)

    g_a = grad_a[...]
    for m in range(2):
        new[m] = 0.95 * fac[m] + (0.05 / width) * dg(g_a, g_a, 1 - m, 1 - m)
    pump()
    for m in range(2):
        t_ref[m] = dot3(split(bas[m]), split(new[m]), 0, 1)
    pump()
    for m in range(2):
        s = split(t_ref[m])
        a_ref[m] = dot3(s, s, 1, 1)
    pump()
    orthonormal(a_ref, t_ref, e_ref, pump)
    pump(len(todo))
    to_owners(out_b, grad, give_b, take_b, group - 1)

    block = order_ref[z * group + f]
    flag = lax.fori_loop(
        0, nref, lambda i, c: c | (ids_ref[i] == block).astype(jnp.int32), jnp.int32(0)
    )
    refreshed = jnp.full((width, width), flag, jnp.int32) == 1
    for m, q in enumerate((lq, rq)):
        q[0], q[1] = split(jnp.where(refreshed, t_ref[m].T, bas[m]))
    left = (lq[0], lq[1])
    right = (rq[0], rq[1])
    rotated[...] = 0.9 * dot3(split(dot3(left, split(mom[...]), 0, 0)), right)
    from_all(out_b, grad, give_b, take_b)

    g = grad[...]
    turned = (dg(left[0], g, 0, 0) + dg(left[1], g, 0, 0)).astype(bf16)
    rot_grad = dg(turned, right[0]) + dg(turned, right[1])
    second = 0.95 * sec[...] + 0.05 * rot_grad * rot_grad
    scaled = ((rotated[...] + 0.1 * rot_grad) / (jnp.sqrt(second) + 1e-08)).astype(bf16)
    back_hi[...] = (dg(left[0], scaled) + dg(left[1], scaled)).astype(bf16)

    quarter = nf // 4

    def give_back(peer):
        there = pl.ds(pl.multiple_of(peer * rows, rows), rows)
        i = lax.rem(peer - f + nf, nf)
        return pltpu.make_async_remote_copy(
            src_ref=update.at[there],
            dst_ref=held.at[f],
            send_sem=give_c.at[i],
            recv_sem=take_c.at[i],
            device_id=(z, peer),
            device_id_type=MESH,
        )

    def some_rows(r, c):
        at = lax.rem(f // quarter + r, 4)
        span = pl.ds(pl.multiple_of(at * quarter * rows, quarter * rows), quarter * rows)
        chunk = back_hi[span]
        update[span] = (dg(chunk, rq[0], 1, 1) + dg(chunk, rq[1], 1, 1)).astype(bf16)

        def one(i, c):
            peer = at * quarter + lax.rem(f + i, quarter)

            @pl.when(peer != f)
            def _():
                give_back(peer).start()

            return c

        lax.fori_loop(0, quarter, one, 0)
        return c

    lax.fori_loop(0, 4, some_rows, 0)
    held[f] = update[mine]

    ring_sent(ring_a, 1)
    ring_sent(ring_b, pieces)

    def drain(i, c):
        give(out_a, grad_a, give_a, take_a, i).wait_send()
        give(out_b, grad, give_b, take_b, i).wait_send()
        peer = lax.rem(f + i, nf)
        give_back(peer).wait_send()
        give_back(peer).wait_recv()
        return c

    lax.fori_loop(1, nf, drain, 0)


def main(nz, nf, order, ids, parts, *rest):
    _, blocks, rows, width = parts.shape
    group = blocks // nz
    smem = pl.BlockSpec(memory_space=pltpu.SMEM)
    vmem = pl.BlockSpec(memory_space=pltpu.VMEM)
    hbm = pl.BlockSpec(memory_space=pl.ANY)
    square = pltpu.VMEM((width, width), f32)
    pair = pltpu.VMEM((2, width, width), f32)
    pair16 = pltpu.VMEM((2, width, width), bf16)
    square16 = pltpu.VMEM((width, width), bf16)
    slots = pltpu.VMEM((nf, rows, width), bf16)
    half_a, half_b = EARLY // 2, (group - EARLY) // 2
    ring = pltpu.SemaphoreType.DMA
    return pl.pallas_call(
        functools.partial(main_kernel, nz, nf),
        out_shape=(
            jax.ShapeDtypeStruct((nf, rows, width), bf16),
            jax.ShapeDtypeStruct((width, width), bf16),
        ),
        in_specs=[smem, smem] + [hbm] * 7,
        out_specs=(vmem, vmem),
        scratch_shapes=[
            pltpu.VMEM((blocks, rows, width), bf16),
            pltpu.VMEM((2, 2, half_a, rows, width), bf16),
            pltpu.VMEM((2, 2, 4, half_a, rows, width), bf16),
            pltpu.VMEM((2, 2, half_b, rows, width), bf16),
            pltpu.VMEM((2, 2, 4, half_b, rows, width), bf16),
            slots,
            slots,
            square16,
            slots,
            square16,
            pair,
            pair,
            pair,
            pair,
            pair,
            square,
            square,
            square,
            pair16,
            pair16,
            pltpu.VMEM((2, NB, 2 * NB), f32),
            square16,
            ring((nz + 6,)),
            ring((2, 2, 4, half_a // PER)),
            ring((2, 2, 4, half_a // PER)),
            ring((2, 2, 4, half_b // PER)),
            ring((2, 2, 4, half_b // PER)),
            ring((nf,)),
            ring((nf,)),
            ring((nf,)),
            ring((nf,)),
            ring((nf,)),
            ring((nf,)),
        ],
        compiler_params=pltpu.CompilerParams(
            collective_id=0, has_side_effects=True, vmem_limit_bytes=59 * 2**20
        ),
        name="soap_step",
    )(order, ids, parts, *rest)


def tail_kernel(nz, nf, order_ref, held, grad_ref, lf_ref, rf_ref, out_hbm, ln_hbm, rn_hbm, new, sem):
    z = lax.axis_index("replica")
    width = grad_ref.shape[1]
    group = held.shape[0]

    def place(i):
        block = jnp.clip(order_ref[z * group + i] - z * group, 0, group - 1)
        return pltpu.make_async_copy(held.at[i], out_hbm.at[block], sem.at[2 + i])

    def begin(i, c):
        place(i).start()
        return c

    def end(i, c):
        place(i).wait()
        return c

    lax.fori_loop(0, nf, begin, 0)
    grad = grad_ref[...]
    stores = []
    for m, (fac, hbm) in enumerate(((lf_ref, ln_hbm), (rf_ref, rn_hbm))):
        new[m] = 0.95 * fac[0] + (0.05 / width) * dg(grad, grad, 1 - m, 1 - m)
        stores.append(pltpu.make_async_copy(new.at[m], hbm.at[0], sem.at[m]))
        stores[m].start()
    for store in stores:
        store.wait()
    lax.fori_loop(0, nf, end, 0)


def tail(nz, nf, order, held, grad, lf, rf):
    width = grad.shape[1]
    smem = pl.BlockSpec(memory_space=pltpu.SMEM)
    vmem = pl.BlockSpec(memory_space=pltpu.VMEM)
    hbm = pl.BlockSpec(memory_space=pl.ANY)
    whole = jax.ShapeDtypeStruct((1, width, width), f32)
    return pl.pallas_call(
        functools.partial(tail_kernel, nz, nf),
        out_shape=(jax.ShapeDtypeStruct(held.shape, bf16), whole, whole),
        in_specs=[smem, vmem, vmem, vmem, vmem],
        out_specs=(hbm, hbm, hbm),
        scratch_shapes=[
            pltpu.VMEM((2, width, width), f32),
            pltpu.SemaphoreType.DMA((2 + nf,)),
        ],
        compiler_params=pltpu.CompilerParams(vmem_limit_bytes=16 * 2**20),
        name="write_out",
    )(order, held, grad, lf, rf)


def solution(mesh):
    nz, nf = mesh.shape["replica"], mesh.shape["fsdp"]

    def on_device(parts, moment, second, lf, rf, lb, rb, order, ids):
        held, grad = main(nz, nf, order, ids, parts, moment, second, lf, rf, lb, rb)
        return tail(nz, nf, order, held, grad, lf, rf)

    placed = (P("replica", None, "fsdp", None),) + (P(("replica", "fsdp"), None, None),) * 6 + (P(), P())
    return jax.shard_map(
        on_device,
        mesh=mesh,
        in_specs=placed,
        out_specs=(
            P("replica", "fsdp", None),
            P(("replica", "fsdp"), None, None),
            P(("replica", "fsdp"), None, None),
        ),
        check_vma=False,
    )
```

time: 559 us -> 99.9 us (0.18); the launches traced: 551 us -> 99.7 us
  starting transfers between devices: 320 us -> 0 us
  blocking collectives: 103 us -> 0 us
  Pallas kernels: 0 us -> 96.7 us
  waiting for transfers between devices: 60.5 us -> 0 us
  matrix products: 21.9 us -> 0 us
  other arithmetic: 16.3 us -> 0 us
  loops' own time: 14 us -> 0 us
  local copies, waits for them, and re-layouts: 13.1 us -> 2.09 us
    all_to_all x2 -> x0, starting transfers between devices: 320 us -> none  [the longest x1 311 us: on_device(): lax.all_to_all(update, 'fsdp', split_axis=1, concat_axis=0, tiled=True)]
    all_to_all x1 -> x0, blocking collectives: 103 us -> none  [on_device(): lax.all_to_all(arranged, 'replica', split_axis=1, concat_axis=0, tiled=True)]
    pallas_call x0 -> x2, Pallas kernels: none -> 96.7 us  [the longest x1 93.6 us: main(): pl.pallas_call(functools.partial(main_kernel, nz, nf), out_shape=(jax.Sha...]
    all_to_all x2 -> x0, waiting for transfers between devices: 60.5 us -> none  [the longest x1 48.9 us: on_device(): lax.all_to_all(lax.all_to_all(arranged, 'replica', split_axis=1, concat_a...]
    dot_general x8 -> x0, matrix products: 21.9 us -> none  [the longest x1 3.17 us: soap_update(): jnp.einsum('kil,klm->kim', jnp.einsum('kji,kjl->kil', left_q, gradient, p...]
    another operation x2 -> x0, loops' own time: 14 us -> none  [single(): lax.cond(flag_one, lambda: orthonormal(jnp.dot(factor_one, basis_one, pre...]
  transfers between devices with their start and end apart: 2 -> 0, of which waited for: 2 -> 0; matrix products, arithmetic and copies ran while one was open for 0% -> 0% of each run, Pallas kernels for 0% -> 0%
where the time goes in v2:
time: 99.9 us; the launch traced here: 99.7 us
  Pallas kernels  96.7 us (97%)
  local copies, waits for them, and re-layouts  2.09 us (2%)
    pallas_call x1, Pallas kernels, main(): pl.pallas_call(functools.partial(main_kernel, nz, nf), out_shape=(jax.Sha...  93.6 us
    pallas_call x1, Pallas kernels, tail(): pl.pallas_call(functools.partial(tail_kernel, nz, nf), out_shape=(jax.Sha...  3.13 us
    unnamed x10, local copies, waits for them, and re-layouts  2.09 us

profile of v2, /device:TPU:1, one launch (start us, length us, event | category | flops | bytes accessed | tf_op | source)
XLA Modules:
  0.0 99.7 jit_solution(8335051850079028773)
XLA Ops:
  0.6 0.0 copy-start.4
  0.6 0.0 copy-start.1
  0.7 0.0 copy-start
  0.7 93.6 %soap_step.1 = (bf16[32,16,512]{2,1,0:T(8,128)(2,1)}, bf16[512,512]{1,0:T(8,128)(2,1)}) custom-call(s32[256]{0:T(256)} %order_ref.3, s32[25]{0:T(128)} %ids_ref.1, bf16[1,256,16,512]{3,2,1,0:T(8,128)(2,1)} %parts_hbm.1, f32[1,512,512]{2,1,0:T(8,128)} %mom_hbm.1, f32[1,512,512]{2,1,0:T(8,128)} %sec_hbm.1, f32[1,512,512]{2,1,0:T(8,128)} %lf_ref.1, ...), custom_call_target="tpu_custom_call" | custom-call | tf_op jit(solution)/shard_map/soap_step/pallas_call | solution.py:409
  94.3 0.0 copy-done.4
  94.3 0.0 copy-done.1
  94.3 0.0 copy-done
  94.3 0.0 copy-start.2
  94.3 1.0 %copy-done.2 = bf16[32,16,512]{2,1,0:T(8,128)(2,1)S(1)} copy-done((bf16[32,16,512]{2,1,0:T(8,128)(2,1)S(1)}, bf16[32,16,512]{2,1,0:T(8,128)(2,1)}, u32[]{:S(2)}) %copy-start.2) | copy-done | bytes 524312
  95.3 0.0 copy-start.3
  95.3 1.0 %copy-done.3 = bf16[512,512]{1,0:T(8,128)(2,1)S(1)} copy-done((bf16[512,512]{1,0:T(8,128)(2,1)S(1)}, bf16[512,512]{1,0:T(8,128)(2,1)}, u32[]{:S(2)}) %copy-start.3) | copy-done | bytes 524312
  96.4 3.1 %write_out.1 = (bf16[32,16,512]{2,1,0:T(8,128)(2,1)}, f32[1,512,512]{2,1,0:T(8,128)}, f32[1,512,512]{2,1,0:T(8,128)}) custom-call(s32[256]{0:T(256)S(1)} %copy-done.4, bf16[32,16,512]{2,1,0:T(8,128)(2,1)S(1)} %copy-done.2, bf16[512,512]{1,0:T(8,128)(2,1)S(1)} %copy-done.3, f32[1,512,512]{2,1,0:T(8,128)S(1)} %copy-done, f32[1,512,512]{2,1,0:T(8,128)S(1)} %copy-done.1), custom_call_target="tpu_custom_call" | custom-call | tf_op jit(solution)/shard_map/write_out/pallas_call | solution.py:494
Async XLA Ops:
  0.6 93.6 %copy-start.4 = (s32[256]{0:T(256)S(1)}, s32[256]{0:T(256)}, u32[]{:S(2)}) copy-start(s32[256]{0:T(256)} %order_ref.3) | copy-start | bytes 3076
  0.6 93.6 %copy-start.1 = (f32[1,512,512]{2,1,0:T(8,128)S(1)}, f32[1,512,512]{2,1,0:T(8,128)}, u32[]{:S(2)}) copy-start(f32[1,512,512]{2,1,0:T(8,128)} %rf_ref.1) | copy-start | bytes 3145732
  0.7 93.6 %copy-start = (f32[1,512,512]{2,1,0:T(8,128)S(1)}, f32[1,512,512]{2,1,0:T(8,128)}, u32[]{:S(2)}) copy-start(f32[1,512,512]{2,1,0:T(8,128)} %lf_ref.1) | copy-start | bytes 3145732
  94.3 1.0 %copy-start.2 = (bf16[32,16,512]{2,1,0:T(8,128)(2,1)S(1)}, bf16[32,16,512]{2,1,0:T(8,128)(2,1)}, u32[]{:S(2)}) copy-start(bf16[32,16,512]{2,1,0:T(8,128)(2,1)} %get-tuple-element.5.held) | copy-start | bytes 1572868
  95.3 1.0 %copy-start.3 = (bf16[512,512]{1,0:T(8,128)(2,1)S(1)}, bf16[512,512]{1,0:T(8,128)(2,1)}, u32[]{:S(2)}) copy-start(bf16[512,512]{1,0:T(8,128)(2,1)} %get-tuple-element.6.grad_ref) | copy-start | bytes 1572868

commit v3 on v2

--- a/solution.py
+++ b/solution.py
@@ -82,48 +82,74 @@
             e_ref[m, at : at + 8, :] = piv
 
 
-def orthonormal(a_ref, t_ref, e_ref, between):
+def orthonormal(a_ref, t_ref, e_ref, w_ref, u_ref, between):
     size = a_ref.shape[1]
     eye = (
         lax.broadcasted_iota(jnp.int32, (NB, NB), 0) == lax.broadcasted_iota(jnp.int32, (NB, NB), 1)
     ).astype(f32)
+
+    def block(m, at):
+        e_ref[m, :, :NB] = a_ref[m, at : at + NB, at : at + NB]
+        e_ref[m, :, NB:] = eye
+
+    def rest(m, o):
+        n, c = o + NB, (o + NB) // 128 * 128
+        t = dot3((w_ref[m, 0], w_ref[m, 1]), split(t_ref[m, o:n, :]))
+        t_ref[m, o:n, :] = t
+        if n < size:
+            u = u_ref[m, 0, :, c:], u_ref[m, 1, :, c:]
+            t_ref[m, n:, :] = t_ref[m, n:, :] - dot3(u, split(t), 0, 0)[n - c :]
+            for r in range(c, size, 128):
+                top = max(r, n)
+                strip = u_ref[m, 0, :, r : r + 128], u_ref[m, 1, :, r : r + 128]
+                right = u_ref[m, 0, :, r:], u_ref[m, 1, :, r:]
+                change = dot3(strip, right, 0, 0)[top - r :]
+                a_ref[m, top : r + 128, r:] = a_ref[m, top : r + 128, r:] - change
+
+    for m in range(2):
+        block(m, 0)
     for o in range(0, size, NB):
-        n = o + NB
-        for m in range(2):
-            e_ref[m, :, :NB] = a_ref[m, o:n, o:n]
-            e_ref[m, :, NB:] = eye
+        n, c = o + NB, (o + NB) // 128 * 128
         chol_inverse(e_ref)
-        between()
+        if o > 0:
+            for m in range(2):
+                rest(m, o - NB)
+        between(2)
         for m in range(2):
             w = split(e_ref[m, :, NB:])
-            t = dot3(w, split(t_ref[m, o:n, :]))
-            t_ref[m, o:n, :] = t
+            w_ref[m, 0], w_ref[m, 1] = w
             if n < size:
-                u = split(dot3(w, split(a_ref[m, o:n, n:])))
-                a_ref[m, n:, n:] = a_ref[m, n:, n:] - dot3(u, u, 0, 0)
-                t_ref[m, n:, :] = t_ref[m, n:, :] - dot3(u, split(t), 0, 0)
+                u = split(dot3(w, split(a_ref[m, o:n, c:])))
+                u_ref[m, 0, :, c:], u_ref[m, 1, :, c:] = u
+                part = tuple(x[:, n - c : n - c + NB] for x in u)
+                e_ref[m, :, :NB] = a_ref[m, n : n + NB, n : n + NB] - dot3(part, part, 0, 0)
+                e_ref[m, :, NB:] = eye
         between()
+    for m in range(2):
+        rest(m, size - NB)
 
 
 def main_kernel(
     nz, nf, order_ref, ids_ref, parts_hbm, mom_hbm, sec_hbm, lf_hbm, rf_hbm, lb_hbm, rb_hbm,
-    held, grad,
-    own, first_a, arms_a, first_b, arms_b, acc, out_a, grad_a, out_b, update,
+    held, grad_hbm,
+    own_0, own_1, own_2, own_3, own_4, own_5, own_6, own_7, first_a, arms_a, first_b, arms_b, acc, out_a, grad_a, out_b, update,
     fac, bas, new, a_ref, t_ref, mom, sec, rotated, lq, rq, e_ref, back_hi,
-    load_sem, send_a, recv_a, send_b, recv_b, give_a, take_a, give_b, take_b, give_c, take_c,
+    grad, lt, rt, w_ref, u_ref, keep_sem, load_sem, send_a, recv_a, send_b, recv_b, give_a, take_a, give_b, take_b, give_c, take_c,
 ):
     z = lax.axis_index("replica")
     f = lax.axis_index("fsdp")
-    group = own.shape[0] // nz
-    rows, width = own.shape[1:]
+    own = (own_0, own_1, own_2, own_3, own_4, own_5, own_6, own_7)
+    group, rows, width = own_0.shape
     nref = ids_ref.shape[0]
 
     loads = [
         pltpu.make_async_copy(
-            parts_hbm.at[0, pl.ds(g * group, group)], own.at[pl.ds(g * group, group)], load_sem.at[g]
+            parts_hbm.at[0, pl.ds(lax.rem(z + k, nz) * group, group)], own[k], load_sem.at[k]
         )
-        for g in range(nz)
+        for k in range(nz)
     ]
+    first_needed = (4, 3, 5)
+    then_needed = (2, 6, 1, 7, 0)
     places = (
         (lf_hbm, fac.at[0]),
         (rf_hbm, fac.at[1]),
@@ -136,8 +162,8 @@
         pltpu.make_async_copy(src.at[0], dst, load_sem.at[nz + n])
         for n, (src, dst) in enumerate(places)
     ]
-    for load in loads + later:
-        load.start()
+    for k in first_needed + then_needed:
+        loads[k].start()
 
     barrier = pltpu.get_barrier_semaphore()
     for step in (1, nz - 1):
@@ -176,19 +202,19 @@
         same = sum((a == block).astype(jnp.int32) for a in own_early)
         return jnp.where(same > 0, below, EARLY + block - below)
 
-    for load in loads:
-        load.wait()
+    for k in first_needed:
+        loads[k].wait()
     pl.semaphore_wait(barrier, nf + 1)
 
     def target(way, arm, hop):
         left = HOPS[arm] - hop
-        return lax.rem(z + (nz - left if way == DOWN else left), nz)
+        return nz - left if way == DOWN else left
 
     def ring_copy(stage, way, arm, hop, p):
-        first, arms, send, recv = stage
+        first, arms, send, recv, per = stage
         src = first.at[way, arm] if hop == 0 else arms.at[way, arm, hop - 1]
         step = nz - 1 if way == DOWN else 1
-        piece = pl.ds(p * PER, PER)
+        piece = pl.ds(p * per, per)
         return pltpu.make_async_remote_copy(
             src_ref=src.at[piece],
             dst_ref=arms.at[way, arm, hop].at[piece],
@@ -198,14 +224,14 @@
             device_id_type=MESH,
         )
 
-    def block_at(stage, dest, part, i):
-        found = early(dest)
+    def block_at(stage, k, part, i):
+        found = early(lax.rem(z + k, nz))
         if stage is ring_a:
-            return dest * group + found[part * (EARLY // 2) + i]
-        return dest * group + late(found, part * ((group - EARLY) // 2) + i)
+            return found[part * (EARLY // 2) + i]
+        return late(found, part * ((group - EARLY) // 2) + i)
 
     def ring_step(stage, hop, p):
-        first, arms = stage[:2]
+        first, arms, per = stage[0], stage[1], stage[4]
         for arm in (LONG, SHORT):
             if hop >= HOPS[arm]:
                 continue
@@ -213,9 +239,9 @@
                 if hop > 0:
                     ring_copy(stage, way, arm, hop - 1, p).wait_recv()
                 dest = target(way, arm, hop)
-                for k in range(PER):
-                    i = p * PER + k
-                    value = own[block_at(stage, dest, way ^ arm, i)]
+                for k in range(per):
+                    i = p * per + k
+                    value = own[dest][block_at(stage, dest, way ^ arm, i)]
                     if hop == 0:
                         first[way, arm, i] = value
                     else:
@@ -224,19 +250,19 @@
                 ring_copy(stage, way, arm, hop, p).start()
 
     def ring_end(stage, p):
-        arms = stage[1]
+        arms, per = stage[1], stage[4]
         base = 0 if stage is ring_a else EARLY
         count = EARLY // 2 if stage is ring_a else (group - EARLY) // 2
         for part in range(2):
             long_way, short_way = (DOWN, UP) if part == 0 else (UP, DOWN)
             ring_copy(stage, long_way, LONG, 3, p).wait_recv()
             ring_copy(stage, short_way, SHORT, 2, p).wait_recv()
-            for k in range(PER):
-                i = p * PER + k
+            for k in range(per):
+                i = p * per + k
                 total = (
                     arms[long_way, LONG, 3, i].astype(f32)
                     + arms[short_way, SHORT, 2, i].astype(f32)
-                    + own[block_at(stage, z, part, i)].astype(f32)
+                    + own[0][block_at(stage, 0, part, i)].astype(f32)
                 )
                 acc[base + part * count + i] = total.astype(bf16)
 
@@ -252,11 +278,12 @@
 
                         lax.fori_loop(0, pieces, sent, 0)
 
-    ring_a = (first_a, arms_a, send_a, recv_a)
-    ring_b = (first_b, arms_b, send_b, recv_b)
+    ring_a = (first_a, arms_a, send_a, recv_a, 1)
+    ring_b = (first_b, arms_b, send_b, recv_b, PER)
     pieces = (group - EARLY) // 2 // PER
     todo = [functools.partial(ring_step, ring_b, hop, p) for hop in range(4) for p in range(pieces)]
     todo += [functools.partial(ring_end, ring_b, p) for p in range(pieces)]
+    todo.append(lambda: to_owners(out_b, grad, give_b, take_b, group - 1))
     todo.reverse()
 
     def pump(n=1):
@@ -295,17 +322,19 @@
 
         lax.fori_loop(1, nf, one, 0)
 
-    ring_step(ring_a, 0, 0)
-    pump(2)
-    ring_step(ring_a, 1, 0)
-    pump(1)
-    ring_step(ring_a, 2, 0)
-    pump(2)
-    ring_step(ring_a, 3, 0)
-    pump(2)
-    ring_end(ring_a, 0)
+    for hop in range(4):
+        for p in range(EARLY // 2):
+            ring_step(ring_a, hop, p)
+        pump(2 if hop else 1)
+        if hop == 0:
+            for k in then_needed:
+                loads[k].wait()
+            for load in later:
+                load.start()
+    for p in range(EARLY // 2):
+        ring_end(ring_a, p)
     to_owners(out_a, grad_a, give_a, take_a, EARLY - 1)
-    pump(4)
+    pump(5)
     for load in later:
         load.wait()
     from_all(out_a, grad_a, give_a, take_a)
@@ -321,28 +350,29 @@
         s = split(t_ref[m])
         a_ref[m] = dot3(s, s, 1, 1)
     pump()
-    orthonormal(a_ref, t_ref, e_ref, pump)
+    orthonormal(a_ref, t_ref, e_ref, w_ref, u_ref, pump)
     pump(len(todo))
-    to_owners(out_b, grad, give_b, take_b, group - 1)
 
     block = order_ref[z * group + f]
     flag = lax.fori_loop(
         0, nref, lambda i, c: c | (ids_ref[i] == block).astype(jnp.int32), jnp.int32(0)
     )
     refreshed = jnp.full((width, width), flag, jnp.int32) == 1
-    for m, q in enumerate((lq, rq)):
+    for m, (q, t) in enumerate(((lq, lt), (rq, rt))):
         q[0], q[1] = split(jnp.where(refreshed, t_ref[m].T, bas[m]))
-    left = (lq[0], lq[1])
-    right = (rq[0], rq[1])
-    rotated[...] = 0.9 * dot3(split(dot3(left, split(mom[...]), 0, 0)), right)
+        t[0], t[1] = split(jnp.where(refreshed, t_ref[m], bas[m].T))
+    half = split(dot3((lt[0], lt[1]), split(mom[...])))
+    rotated[...] = 0.9 * dot3(half, (rq[0], rq[1]))
     from_all(out_b, grad, give_b, take_b)
+    keep = pltpu.make_async_copy(grad, grad_hbm, keep_sem.at[0])
+    keep.start()
 
     g = grad[...]
-    turned = (dg(left[0], g, 0, 0) + dg(left[1], g, 0, 0)).astype(bf16)
-    rot_grad = dg(turned, right[0]) + dg(turned, right[1])
+    turned = (dg(lt[0], g) + dg(lt[1], g)).astype(bf16)
+    rot_grad = dg(turned, rq[0]) + dg(turned, rq[1])
     second = 0.95 * sec[...] + 0.05 * rot_grad * rot_grad
     scaled = ((rotated[...] + 0.1 * rot_grad) / (jnp.sqrt(second) + 1e-08)).astype(bf16)
-    back_hi[...] = (dg(left[0], scaled) + dg(left[1], scaled)).astype(bf16)
+    back_hi[...] = (dg(lq[0], scaled) + dg(lq[1], scaled)).astype(bf16)
 
     quarter = nf // 4
 
@@ -362,7 +392,7 @@
         at = lax.rem(f // quarter + r, 4)
         span = pl.ds(pl.multiple_of(at * quarter * rows, quarter * rows), quarter * rows)
         chunk = back_hi[span]
-        update[span] = (dg(chunk, rq[0], 1, 1) + dg(chunk, rq[1], 1, 1)).astype(bf16)
+        update[span] = (dg(chunk, rt[0]) + dg(chunk, rt[1])).astype(bf16)
 
         def one(i, c):
             peer = at * quarter + lax.rem(f + i, quarter)
@@ -377,9 +407,10 @@
         return c
 
     lax.fori_loop(0, 4, some_rows, 0)
-    held[f] = update[mine]
-
-    ring_sent(ring_a, 1)
+    stay = pltpu.make_async_copy(update.at[mine], held.at[f], keep_sem.at[1])
+    stay.start()
+
+    ring_sent(ring_a, EARLY // 2)
     ring_sent(ring_b, pieces)
 
     def drain(i, c):
@@ -391,13 +422,14 @@
         return c
 
     lax.fori_loop(1, nf, drain, 0)
+    stay.wait()
+    keep.wait()
 
 
 def main(nz, nf, order, ids, parts, *rest):
     _, blocks, rows, width = parts.shape
     group = blocks // nz
     smem = pl.BlockSpec(memory_space=pltpu.SMEM)
-    vmem = pl.BlockSpec(memory_space=pltpu.VMEM)
     hbm = pl.BlockSpec(memory_space=pl.ANY)
     square = pltpu.VMEM((width, width), f32)
     pair = pltpu.VMEM((2, width, width), f32)
@@ -413,9 +445,9 @@
             jax.ShapeDtypeStruct((width, width), bf16),
         ),
         in_specs=[smem, smem] + [hbm] * 7,
-        out_specs=(vmem, vmem),
+        out_specs=(hbm, hbm),
         scratch_shapes=[
-            pltpu.VMEM((blocks, rows, width), bf16),
+            *[pltpu.VMEM((group, rows, width), bf16)] * nz,
             pltpu.VMEM((2, 2, half_a, rows, width), bf16),
             pltpu.VMEM((2, 2, 4, half_a, rows, width), bf16),
             pltpu.VMEM((2, 2, half_b, rows, width), bf16),
@@ -437,9 +469,15 @@
             pair16,
             pltpu.VMEM((2, NB, 2 * NB), f32),
             square16,
+            square16,
+            pair16,
+            pair16,
+            pltpu.VMEM((2, 2, NB, NB), bf16),
+            pltpu.VMEM((2, 2, NB, width), bf16),
+            ring((2,)),
             ring((nz + 6,)),
-            ring((2, 2, 4, half_a // PER)),
-            ring((2, 2, 4, half_a // PER)),
+            ring((2, 2, 4, half_a)),
+            ring((2, 2, 4, half_a)),
             ring((2, 2, 4, half_b // PER)),
             ring((2, 2, 4, half_b // PER)),
             ring((nf,)),
@@ -456,14 +494,18 @@
     )(order, ids, parts, *rest)
 
 
-def tail_kernel(nz, nf, order_ref, held, grad_ref, lf_ref, rf_ref, out_hbm, ln_hbm, rn_hbm, new, sem):
+def tail_kernel(nz, nf, order_ref, held, grad_hbm, lf_ref, rf_ref, out_hbm, ln_hbm, rn_hbm, grad_ref, rows, new, sem):
     z = lax.axis_index("replica")
     width = grad_ref.shape[1]
     group = held.shape[0]
+    fetch = pltpu.make_async_copy(held, rows, sem.at[3 + nf])
+    fetch.start()
+    load = pltpu.make_async_copy(grad_hbm, grad_ref, sem.at[2 + nf])
+    load.start()
 
     def place(i):
         block = jnp.clip(order_ref[z * group + i] - z * group, 0, group - 1)
-        return pltpu.make_async_copy(held.at[i], out_hbm.at[block], sem.at[2 + i])
+        return pltpu.make_async_copy(rows.at[i], out_hbm.at[block], sem.at[2 + i])
 
     def begin(i, c):
         place(i).start()
@@ -473,7 +515,9 @@
         place(i).wait()
         return c
 
+    fetch.wait()
     lax.fori_loop(0, nf, begin, 0)
+    load.wait()
     grad = grad_ref[...]
     stores = []
     for m, (fac, hbm) in enumerate(((lf_ref, ln_hbm), (rf_ref, rn_hbm))):
@@ -494,13 +538,15 @@
     return pl.pallas_call(
         functools.partial(tail_kernel, nz, nf),
         out_shape=(jax.ShapeDtypeStruct(held.shape, bf16), whole, whole),
-        in_specs=[smem, vmem, vmem, vmem, vmem],
+        in_specs=[smem, hbm, hbm, vmem, vmem],
         out_specs=(hbm, hbm, hbm),
         scratch_shapes=[
+            pltpu.VMEM((width, width), bf16),
+            pltpu.VMEM(held.shape, bf16),
             pltpu.VMEM((2, width, width), f32),
-            pltpu.SemaphoreType.DMA((2 + nf,)),
+            pltpu.SemaphoreType.DMA((4 + nf,)),
         ],
-        compiler_params=pltpu.CompilerParams(vmem_limit_bytes=16 * 2**20),
+        compiler_params=pltpu.CompilerParams(vmem_limit_bytes=63 * 2**20),
         name="write_out",
     )(order, held, grad, lf, rf)
 

time: 99.9 us -> 94.3 us (0.944)
  Pallas kernels: 96.7 us -> 93.3 us
  local copies, waits for them, and re-layouts: 2.09 us -> 0 us
    pallas_call x1, Pallas kernels: 93.6 us -> 88.2 us  [main(): pl.pallas_call(functools.partial(main_kernel, nz, nf), out_shape=(jax.Sha...]
    unnamed x10 -> x0, local copies, waits for them, and re-layouts: 2.09 us -> none
    pallas_call x1, Pallas kernels: 3.13 us -> 5.05 us  [tail(): pl.pallas_call(functools.partial(tail_kernel, nz, nf), out_shape=(jax.Sha...]
where the time goes in v3:
time: 94.3 us; the launch traced here: 94.1 us
  Pallas kernels  93.3 us (99%)
    pallas_call x1, Pallas kernels, main(): pl.pallas_call(functools.partial(main_kernel, nz, nf), out_shape=(jax.Sha...  88.2 us
    pallas_call x1, Pallas kernels, tail(): pl.pallas_call(functools.partial(tail_kernel, nz, nf), out_shape=(jax.Sha...  5.05 us

profile of v3, /device:TPU:1, one launch (start us, length us, event | category | flops | bytes accessed | tf_op | source)
XLA Modules:
  0.0 94.1 jit_solution(10676240820102857961)
XLA Ops:
  0.6 88.2 %soap_step.1 = (bf16[32,16,512]{2,1,0:T(8,128)(2,1)}, bf16[512,512]{1,0:T(8,128)(2,1)}) custom-call(s32[256]{0:T(256)} %order_ref.3, s32[25]{0:T(128)} %ids_ref.1, bf16[1,256,16,512]{3,2,1,0:T(8,128)(2,1)} %parts_hbm.1, f32[1,512,512]{2,1,0:T(8,128)} %mom_hbm.1, f32[1,512,512]{2,1,0:T(8,128)} %sec_hbm.1, f32[1,512,512]{2,1,0:T(8,128)} %lf_ref.1, ...), custom_call_target="tpu_custom_call" | custom-call | tf_op jit(solution)/shard_map/soap_step/pallas_call | solution.py:441
  88.9 5.1 %write_out.1 = (bf16[32,16,512]{2,1,0:T(8,128)(2,1)}, f32[1,512,512]{2,1,0:T(8,128)}, f32[1,512,512]{2,1,0:T(8,128)}) custom-call(s32[256]{0:T(256)} %order_ref.3, bf16[32,16,512]{2,1,0:T(8,128)(2,1)} %get-tuple-element.5.held, bf16[512,512]{1,0:T(8,128)(2,1)} %get-tuple-element.6.grad_hbm, f32[1,512,512]{2,1,0:T(8,128)} %lf_ref.1, f32[1,512,512]{2,1,0:T(8,128)} %rf_ref.1), custom_call_target="tpu_custom_call" | custom-call | tf_op jit(solution)/shard_map/write_out/pallas_call | solution.py:538

commit v4 on v3

--- a/solution.py
+++ b/solution.py
@@ -494,7 +494,7 @@
     )(order, ids, parts, *rest)
 
 
-def tail_kernel(nz, nf, order_ref, held, grad_hbm, lf_ref, rf_ref, out_hbm, ln_hbm, rn_hbm, grad_ref, rows, new, sem):
+def tail_kernel(nz, nf, order_ref, held, grad_hbm, lf_hbm, rf_hbm, out_hbm, ln_hbm, rn_hbm, grad_ref, rows, fac, new, sem):
     z = lax.axis_index("replica")
     width = grad_ref.shape[1]
     group = held.shape[0]
@@ -502,6 +502,12 @@
     fetch.start()
     load = pltpu.make_async_copy(grad_hbm, grad_ref, sem.at[2 + nf])
     load.start()
+    olds = [
+        pltpu.make_async_copy(hbm.at[0], fac.at[m], sem.at[4 + nf + m])
+        for m, hbm in enumerate((lf_hbm, rf_hbm))
+    ]
+    for old in olds:
+        old.start()
 
     def place(i):
         block = jnp.clip(order_ref[z * group + i] - z * group, 0, group - 1)
@@ -520,8 +526,9 @@
     load.wait()
     grad = grad_ref[...]
     stores = []
-    for m, (fac, hbm) in enumerate(((lf_ref, ln_hbm), (rf_ref, rn_hbm))):
-        new[m] = 0.95 * fac[0] + (0.05 / width) * dg(grad, grad, 1 - m, 1 - m)
+    for m, hbm in enumerate((ln_hbm, rn_hbm)):
+        olds[m].wait()
+        new[m] = 0.95 * fac[m] + (0.05 / width) * dg(grad, grad, 1 - m, 1 - m)
         stores.append(pltpu.make_async_copy(new.at[m], hbm.at[0], sem.at[m]))
         stores[m].start()
     for store in stores:
@@ -532,19 +539,19 @@
 def tail(nz, nf, order, held, grad, lf, rf):
     width = grad.shape[1]
     smem = pl.BlockSpec(memory_space=pltpu.SMEM)
-    vmem = pl.BlockSpec(memory_space=pltpu.VMEM)
     hbm = pl.BlockSpec(memory_space=pl.ANY)
     whole = jax.ShapeDtypeStruct((1, width, width), f32)
     return pl.pallas_call(
         functools.partial(tail_kernel, nz, nf),
         out_shape=(jax.ShapeDtypeStruct(held.shape, bf16), whole, whole),
-        in_specs=[smem, hbm, hbm, vmem, vmem],
+        in_specs=[smem, hbm, hbm, hbm, hbm],
         out_specs=(hbm, hbm, hbm),
         scratch_shapes=[
             pltpu.VMEM((width, width), bf16),
             pltpu.VMEM(held.shape, bf16),
             pltpu.VMEM((2, width, width), f32),
-            pltpu.SemaphoreType.DMA((4 + nf,)),
+            pltpu.VMEM((2, width, width), f32),
+            pltpu.SemaphoreType.DMA((6 + nf,)),
         ],
         compiler_params=pltpu.CompilerParams(vmem_limit_bytes=63 * 2**20),
         name="write_out",

time: 94.3 us -> 93.9 us (level)
  no operation moved by 1% of the time
where the time goes in v4:
time: 93.9 us; the launch traced here: 93.7 us
  Pallas kernels  92.9 us (99%)
    pallas_call x1, Pallas kernels, main(): pl.pallas_call(functools.partial(main_kernel, nz, nf), out_shape=(jax.Sha...  88.2 us
    pallas_call x1, Pallas kernels, tail(): pl.pallas_call(functools.partial(tail_kernel, nz, nf), out_shape=(jax.Sha...  4.67 us

profile of v4, /device:TPU:1, one launch (start us, length us, event | category | flops | bytes accessed | tf_op | source)
XLA Modules:
  0.0 93.7 jit_solution(2483253275252896068)
XLA Ops:
  0.6 88.2 %soap_step.1 = (bf16[32,16,512]{2,1,0:T(8,128)(2,1)}, bf16[512,512]{1,0:T(8,128)(2,1)}) custom-call(s32[256]{0:T(256)} %order_ref.3, s32[25]{0:T(128)} %ids_ref.1, bf16[1,256,16,512]{3,2,1,0:T(8,128)(2,1)} %parts_hbm.1, f32[1,512,512]{2,1,0:T(8,128)} %mom_hbm.1, f32[1,512,512]{2,1,0:T(8,128)} %sec_hbm.1, f32[1,512,512]{2,1,0:T(8,128)} %lf_hbm.3, ...), custom_call_target="tpu_custom_call" | custom-call | tf_op jit(solution)/shard_map/soap_step/pallas_call | solution.py:441
  88.9 4.7 %write_out.1 = (bf16[32,16,512]{2,1,0:T(8,128)(2,1)}, f32[1,512,512]{2,1,0:T(8,128)}, f32[1,512,512]{2,1,0:T(8,128)}) custom-call(s32[256]{0:T(256)} %order_ref.3, bf16[32,16,512]{2,1,0:T(8,128)(2,1)} %get-tuple-element.5.held, bf16[512,512]{1,0:T(8,128)(2,1)} %get-tuple-element.6.grad_hbm, f32[1,512,512]{2,1,0:T(8,128)} %lf_hbm.3, f32[1,512,512]{2,1,0:T(8,128)} %rf_hbm.3), custom_call_target="tpu_custom_call" | custom-call | tf_op jit(solution)/shard_map/write_out/pallas_call | solution.py:544
